TPU v7x, 128 devices: a whole 4x4x4 slice. The times are simulated.
128 devices in a mesh: dp: 16 (over z, x_hi, core), tensor: 8 (over y, x_lo).
Axes of the slice: x: 4 (x_hi: 2, x_lo: 2; x = x_hi * 2 + x_lo), y: 4, z: 4, core: 2. Of those that a mesh axis runs over, the one named last changes fastest.
Arguments:
- query_states: bfloat16 [16, 512, 8192], P('dp', None, 'tensor'), may hold values from -110 to 110
- key_states: bfloat16 [16, 512, 1024], P('dp', None, 'tensor'), may hold values from -4 to 4
- value_states: bfloat16 [16, 512, 1024], P('dp', None, 'tensor'), may hold values from -6 to 6
- segment_ids: int32 [16, 512], P('dp', 'tensor'), may hold values from 0 to 7, never falling along the last dimension, each value on 1 to 256 neighbouring positions
- pair_margins: float32 [16, 4], P('dp'), may hold values from -6 to 6
- upstream: bfloat16 [16, 512, 8192], P('dp', 'tensor'), may hold values from -6 to 6
- out_weight: bfloat16 [8192, 8192], P('tensor', 'dp'), may hold values from -0.0625 to 0.0625
Outputs:
- query_grad: bfloat16 [16, 512, 8192], P('dp', None, 'tensor')
- key_grad: bfloat16 [16, 512, 1024], P('dp', None, 'tensor')
- value_grad: bfloat16 [16, 512, 1024], P('dp', None, 'tensor')
- out_weight_grad: float32 [8192, 8192], P('tensor', 'dp')
Inputs may be any that keep to these rules, and one draw needn't show every extreme that they name: `segment_ids`: every row holds all 8 responses, each of 1 to 256 positions in order.
All inputs are finite; a program needn't handle non-finite values.
Results may differ from a plain program's by a relative error of at most 0.015.
Values may be sent and summed in bfloat16 or wider, within the bound.
No kernel may reach another device: no remote copies, remote signals or barrier semaphores. Data moves between devices by JAX's collectives and lax.ppermute only.
A program may use at most 128 MiB of HBM per device.

v0:
```python
import jax
import jax.numpy as jnp
from jax import lax
from jax.sharding import PartitionSpec as P

HEADS = 64
KV_HEADS = 8
HD = 128


def shards(query_states, key_states, value_states, segment_ids, pair_margins, upstream, out_weight):
    row_count, seq_local, model_width = upstream.shape
    length = query_states.shape[1]
    head_width = query_states.shape[2]
    kv_local = key_states.shape[2] // HD
    group_size = HEADS // KV_HEADS
    score_scale = HD ** (-0.5)
    whole_segs = lax.all_gather(segment_ids, "tensor", axis=1, tiled=True)
    sigma = jax.nn.sigmoid(-pair_margins)
    onehot = (
        segment_ids[:, :, None] // 2 == jnp.arange(sigma.shape[1], dtype=jnp.int32)[None, None, :]
    ).astype(jnp.float32)
    coeff = jnp.sum(onehot * sigma[:, None, :], axis=2)
    signs = jnp.where(segment_ids % 2 == 0, -1.0, 1.0).astype(jnp.float32)
    output_grad = (upstream.astype(jnp.float32) * (signs * coeff)[:, :, None]).astype(jnp.bfloat16)
    weight_full = lax.all_gather(out_weight, "dp", axis=1, tiled=True)
    query_heads = query_states.reshape(row_count, length, kv_local, group_size, HD)
    key_heads = key_states.reshape(row_count, length, kv_local, HD)
    value_heads = value_states.reshape(row_count, length, kv_local, HD)
    position = jnp.arange(length, dtype=jnp.int32)
    allowed = (whole_segs[:, :, None] == whole_segs[:, None, :]) & (
        position[None, None, :] <= position[None, :, None]
    )
    scores = (
        jnp.einsum("rigmd,rjgd->rgmij", query_heads, key_heads, preferred_element_type=jnp.float32)
        * score_scale
    )
    scores = jnp.where(allowed[:, None, None], scores, -1e30)
    highest = jnp.max(scores, axis=-1, keepdims=True)
    expo = jnp.exp(scores - highest)
    probs = expo / jnp.sum(expo, axis=-1, keepdims=True)
    probs_low = probs.astype(jnp.bfloat16)
    attn_out = jnp.einsum(
        "rgmij,rjgd->rigmd", probs_low, value_heads, preferred_element_type=jnp.float32
    )
    attn_out = attn_out.astype(jnp.bfloat16).reshape(row_count, length, head_width)
    block_grad = lax.all_gather(output_grad, "tensor", axis=1, tiled=True)
    partial_value = jnp.einsum(
        "rte,he->rth", block_grad, weight_full, preferred_element_type=jnp.float32
    )
    wgrad_acc = jnp.einsum("rth,rte->he", attn_out, block_grad, preferred_element_type=jnp.float32)
    weight_grad = lax.psum_scatter(
        wgrad_acc.astype(jnp.bfloat16), "dp", scatter_dimension=1, tiled=True
    ).astype(jnp.float32)
    attn_grad = partial_value.astype(jnp.bfloat16)
    grad_heads = attn_grad.reshape(row_count, length, kv_local, group_size, HD)
    prob_grad = jnp.einsum(
        "rigmd,rjgd->rgmij", grad_heads, value_heads, preferred_element_type=jnp.float32
    )
    delta = jnp.sum(probs * prob_grad, axis=-1, keepdims=True)
    score_grad = (score_scale * probs * (prob_grad - delta)).astype(jnp.bfloat16)
    query_grad = jnp.einsum(
        "rgmij,rjgd->rigmd", score_grad, key_heads, preferred_element_type=jnp.float32
    )
    query_grad = query_grad.astype(jnp.bfloat16).reshape(row_count, length, head_width)
    key_grad = jnp.einsum(
        "rgmij,rigmd->rjgd", score_grad, query_heads, preferred_element_type=jnp.float32
    )
    key_grad = key_grad.astype(jnp.bfloat16).reshape(row_count, length, kv_local * HD)
    value_grad = jnp.einsum(
        "rgmij,rigmd->rjgd", probs_low, grad_heads, preferred_element_type=jnp.float32
    )
    value_grad = value_grad.astype(jnp.bfloat16).reshape(row_count, length, kv_local * HD)
    return (query_grad, key_grad, value_grad, weight_grad)


def solution(mesh):
    in_specs = (
        P("dp", None, "tensor"),
        P("dp", None, "tensor"),
        P("dp", None, "tensor"),
        P("dp", "tensor"),
        P("dp", None),
        P("dp", "tensor", None),
        P("tensor", "dp"),
    )
    out_specs = (
        P("dp", None, "tensor"),
        P("dp", None, "tensor"),
        P("dp", None, "tensor"),
        P("tensor", "dp"),
    )
    return jax.shard_map(shards, mesh=mesh, in_specs=in_specs, out_specs=out_specs, check_vma=False)
```

profile of v0, /device:TPU:1, one launch (start us, length us, event | category | flops | bytes accessed | tf_op | source)
XLA Modules:
  0.0 500.5 jit_solution(11753365866720476348)
XLA Ops:
  7.2 0.7 divide_bitcast_fusion
  7.9 1.2 dynamic-slice
  9.8 0.8 bitcast_dynamic-update-slice_fusion
  10.6 0.7 fusion.30
  11.3 2.4 multiply_convert_fusion
  13.8 0.7 all-gather.5.cloned.1.call-update
  14.6 1.5 copy.43
  16.1 9.9 %all-reduce = s32[512]{0:T(512)S(1)} all-reduce(s32[512]{0:T(512)S(1)} %get-tuple-element.14), channel_id=1, replica_groups=mesh['dp'=16,'tensor'=8] {'tensor'}, use_global_device_ids=true, to_apply=%add | all-reduce | flops 512 | bytes 4096 | tf_op jit(solution)/shard_map/eq | solution.py:31
  26.0 0.2 fusion.20
  26.2 2.0 fusion.8
  28.2 3.2 copy-done.1
  31.4 1.8 fusion.7
  33.2 152.3 %all-gather.3.cloned.1.call-done = bf16[1,512,8192]{2,1,0:T(8,128)(2,1)} async-done(((bf16[1,64,8192]{2,1,0:T(8,128)(2,1)}), bf16[1,512,8192]{2,1,0:T(8,128)(2,1)}) %all-gather.3.cloned.1.call-update) | async-done | bytes 8388624 | tf_op jit(solution)/shard_map/all_gather | solution.py:47
  185.4 122.9 %all-gather.5.cloned.1.call-done = bf16[1024,8192]{1,0:T(8,128)(2,1)} async-done(((bf16[1024,512]{1,0:T(8,128)(2,1)}), bf16[1024,8192]{1,0:T(8,128)(2,1)}) %all-gather.5.cloned.1.call-update) | async-done | bytes 16777232 | tf_op jit(solution)/shard_map/all_gather | solution.py:26
  308.4 14.8 %fusion.10 = bf16[512,1024]{1,0:T(8,128)(2,1)S(1)} fusion(bf16[1024,8192]{1,0:T(8,128)(2,1)} %all-gather.5.cloned.1.call-done, bf16[1,512,8192]{2,1,0:T(8,128)(2,1)} %all-gather.3.cloned.1.call-done), kind=kOutput, calls=%fused_computation.17 | convolution fusion | flops 8590458880 | bytes 26214400 | tf_op jit(solution)/shard_map/rte,he->rth/dot_general | solution.py:48
  323.2 1.3 fusion.17
  324.5 2.1 copy-done.2
  326.6 3.4 convert_bitcast_fusion
  330.0 1.9 copy-done.4
  331.9 0.8 convolution_convert_fusion.1
  332.7 15.3 %convolution_convert_fusion = bf16[1024,8192]{1,0:T(8,128)(2,1)} fusion(bf16[512,1024]{0,1:T(8,128)(2,1)S(1)} %bitcast.143, bf16[1,512,8192]{2,1,0:T(8,128)(2,1)} %all-gather.3.cloned.1.call-done), kind=kOutput, calls=%fused_computation | convolution fusion | flops 8598323200 | bytes 26214400 | tf_op jit(solution)/shard_map/rth,rte->he/dot_general | solution.py:51
  348.0 8.2 %copy.36 = bf16[8,512,512]{2,0,1:T(8,128)(2,1)} copy(bf16[8,512,512]{1,2,0:T(8,128)(2,1)} %copy-done.4) | data formatting | bytes 8388608 | tf_op jit(solution)/shard_map/reshape.39
  356.2 0.3 copy.44
  356.4 10.4 %fusion.9 = bf16[8,512,512]{1,2,0:T(8,128)(2,1)S(1)} fusion(f32[512,8,512]{0,2,1:T(8,128)} %copy-done.3, f32[8,512]{1,0:T(8,128)} %get-tuple-element.13, f32[8,512]{1,0:T(8,128)} %copy-done.7, f32[8,512]{1,0:T(8,128)S(1)} %get-tuple-element.16, f32[512,512,8]{1,0,2:T(8,128)} %copy-done.1, pred[512,512]{0,1:T(8,128)(4,1)S(1)} %fusion.20), kind=kLoop, calls=%fused_computation.14 | loop fusion | flops 16777216 | bytes 21282816 | tf_op jit(solution)/shard_map/reshape.33
  366.8 2.2 copy-done.5
  369.0 0.8 convolution_convert_fusion.2
  369.8 1.3 copy.31
  371.2 3.8 fusion.15
  374.9 0.8 copy.32
  375.7 4.1 fusion.16
  379.8 111.3 %reduce-scatter.2.cloned.1.call-done = bf16[1024,512]{1,0:T(8,128)(2,1)} async-done(((bf16[1024,8192]{1,0:T(8,128)(2,1)}), bf16[1024,512]{1,0:T(8,128)(2,1)}) %reduce-scatter.2.cloned.1.call-update) | async-done | bytes 1048592 | tf_op jit(solution)/shard_map/reduce_scatter | solution.py:52
  491.2 2.8 convert_element_type.89
  (19 shorter events, 0.3 us)
Async XLA Ops:
  7.2 19.0 %copy-start = (bf16[1,512,128]{2,1,0:T(8,128)(2,1)S(1)}, bf16[1,512,128]{2,1,0:T(8,128)(2,1)}, u32[]{:S(2)}) copy-start(bf16[1,512,128]{2,1,0:T(8,128)(2,1)} %param.8) | copy-start | bytes 393220
  7.2 178.3 %all-gather.3.cloned.1.call-start = ((), (), s32[]{:S(2)}) async-start(), calls=%async_computation.1 | async-start | bytes 9437184 | tf_op jit(solution)/shard_map/all_gather | solution.py:47
  13.8 294.6 %all-gather.5.cloned.1.call-start = ((), (), s32[]{:S(2)}) async-start(), calls=%async_computation.2 | async-start | bytes 17825792 | tf_op jit(solution)/shard_map/all_gather | solution.py:26
  14.5 476.6 %reduce-scatter.2.cloned.1.call-start = ((), (), s32[]{:S(2)}) async-start(), calls=%async_computation.3 | async-start | bytes 17825792 | tf_op jit(solution)/shard_map/reduce_scatter | solution.py:52
  28.2 3.2 copy-start.1
  33.2 291.3 %copy-start.7 = (f32[8,512]{1,0:T(8,128)}, f32[8,512]{1,0:T(8,128)S(1)}, u32[]{:S(2)}) copy-start(f32[8,512]{1,0:T(8,128)S(1)} %fusion.7) | copy-start | bytes 49156
  33.2 290.1 %copy-start.6 = (bf16[1,512,128]{2,1,0:T(8,128)(2,1)S(1)}, bf16[1,512,128]{2,1,0:T(8,128)(2,1)}, u32[]{:S(2)}) copy-start(bf16[1,512,128]{2,1,0:T(8,128)(2,1)} %param.9) | copy-start | bytes 393220
  323.2 3.4 copy-start.2
  326.6 3.4 copy-start.3
  330.0 1.9 copy-start.4
  366.8 2.2 copy-start.5
Sparse Core Ops, SparseCore 0:
  13.9 171.5 all-gather.2
  187.8 120.5 all-gather.4
  348.1 143.0 reduce-scatter.1
where the time goes:
time: 501 us
  waiting for transfers between devices  387 us (77%)
  matrix products  42.8 us (9%)
  other arithmetic  23.1 us (5%)
  local copies, waits for them, and re-layouts  22.8 us (5%)
  between operations  14.6 us (3%)
  blocking collectives  9.92 us (2%)
    all_gather x1, waiting for transfers between devices, shards(): block_grad = lax.all_gather(output_grad, 'tensor', axis=1, tiled=True)  152 us
    all_gather x1, waiting for transfers between devices, shards(): weight_full = lax.all_gather(out_weight, 'dp', axis=1, tiled=True)  123 us
    reduce_scatter x1, waiting for transfers between devices, shards(): lax.psum_scatter(wgrad_acc.astype(jnp.bfloat16), 'dp', scatter_dimension=...  111 us
    dot_general x1, matrix products, shards(): jnp.einsum('rth,rte->he', attn_out, block_grad, preferred_element_type=jn...  15.3 us
    dot_general x1, matrix products, shards(): jnp.einsum('rte,he->rth', block_grad, weight_full, preferred_element_type...  14.8 us
    unnamed x22, local copies, waits for them, and re-layouts  14.6 us
    another operation x2, other arithmetic  13.7 us
  transfers between devices with their start and end apart: 3, of which 3 were waited for; matrix products, arithmetic and copies ran while one was open for 7% of the time, Pallas kernels for 0%

commit v1 on v0

--- a/solution.py
+++ b/solution.py
@@ -23,7 +23,9 @@
     coeff = jnp.sum(onehot * sigma[:, None, :], axis=2)
     signs = jnp.where(segment_ids % 2 == 0, -1.0, 1.0).astype(jnp.float32)
     output_grad = (upstream.astype(jnp.float32) * (signs * coeff)[:, :, None]).astype(jnp.bfloat16)
-    weight_full = lax.all_gather(out_weight, "dp", axis=1, tiled=True)
+    weight_full = jnp.concatenate(
+        lax.all_to_all(jnp.stack([out_weight] * lax.axis_size("dp")), "dp", 0, 0), axis=1
+    )
     query_heads = query_states.reshape(row_count, length, kv_local, group_size, HD)
     key_heads = key_states.reshape(row_count, length, kv_local, HD)
     value_heads = value_states.reshape(row_count, length, kv_local, HD)

time: 501 us -> 573 us (1.14)
  blocking collectives: 9.92 us -> 342 us
  waiting for transfers between devices: 387 us -> 115 us
  starting transfers between devices: 0.12 us -> 9.51 us
  local copies, waits for them, and re-layouts: 22.8 us -> 28.8 us
    eq x1, blocking collectives: 9.92 us -> 342 us  [shards(): whole_segs[:, :, None] == whole_segs[:, None, :]]
    all_gather x1, waiting for transfers between devices: 152 us -> 0.02 us  [shards(): block_grad = lax.all_gather(output_grad, 'tensor', axis=1, tiled=True)]
    all_gather x1 -> x0, waiting for transfers between devices: 123 us -> none  [shards(): weight_full = lax.all_gather(out_weight, 'dp', axis=1, tiled=True)]
    all_to_all x0 -> x1, starting transfers between devices: none -> 9.43 us  [shards(): lax.all_to_all(jnp.stack([out_weight] * lax.axis_size('dp')), 'dp', 0, 0)]
    another operation x1 -> x2, local copies, waits for them, and re-layouts: 8.18 us -> 14.1 us
    unnamed x22 -> x31, local copies, waits for them, and re-layouts: 14.6 us -> 14.7 us
  transfers between devices with their start and end apart: 3 -> 3, of which waited for: 3 -> 1; matrix products, arithmetic and copies ran while one was open for 7% -> 6% of each run, Pallas kernels for 0% -> 0%
where the time goes in v1:
time: 573 us
  blocking collectives  342 us (60%)
  waiting for transfers between devices  115 us (20%)
  matrix products  43.3 us (8%)
  local copies, waits for them, and re-layouts  28.8 us (5%)
  other arithmetic  18.9 us (3%)
  between operations  14.9 us (3%)
  starting transfers between devices  9.51 us (2%)
    eq x1, blocking collectives, shards(): whole_segs[:, :, None] == whole_segs[:, None, :]  342 us
    reduce_scatter x1, waiting for transfers between devices, shards(): lax.psum_scatter(wgrad_acc.astype(jnp.bfloat16), 'dp', scatter_dimension=...  115 us
    dot_general x1, matrix products, shards(): jnp.einsum('rth,rte->he', attn_out, block_grad, preferred_element_type=jn...  15.1 us
    dot_general x1, matrix products, shards(): jnp.einsum('rte,he->rth', block_grad, weight_full, preferred_element_type...  14.8 us
    unnamed x31, local copies, waits for them, and re-layouts  14.7 us
    another operation x2, other arithmetic  12.6 us
  transfers between devices with their start and end apart: 3, of which 1 were waited for; matrix products, arithmetic and copies ran while one was open for 6% of the time, Pallas kernels for 0%

profile of v1, /device:TPU:1, one launch (start us, length us, event | category | flops | bytes accessed | tf_op | source)
XLA Modules:
  0.0 572.6 jit_solution(12517092456815908806)
XLA Ops:
  7.2 1.5 copy.35
  8.7 6.0 %stack.2 = bf16[16,1024,512]{1,2,0:T(8,128)(2,1)} broadcast(bf16[1024,512]{0,1:T(8,128)(2,1)S(1)} %copy.35), dimensions={1,2} | broadcast | bytes 17825792 | tf_op jit(solution)/shard_map/stack | solution.py:27
  14.7 9.4 %all-to-all-start = ((bf16[16,1024,512]{1,2,0:T(8,128)(2,1)}), bf16[16,1024,512]{1,2,0:T(8,128)(2,1)}, u32[]{:S(2)}, u32[]{:S(2)}) async-start(bf16[16,1024,512]{1,2,0:T(8,128)(2,1)} %stack.2), calls=%async_computation | async-start | bytes 33554432 | tf_op jit(solution)/shard_map/all_to_all | solution.py:27
  24.2 0.6 dynamic-slice
  25.5 0.1 bitcast_dynamic-update-slice_fusion
  25.6 0.1 select_reduce_fusion
  25.7 1.2 multiply_convert_fusion
  27.0 0.3 copy.52
  27.3 342.0 %all-reduce = s32[512]{0:T(512)S(1)} all-reduce(s32[512]{0:T(512)S(1)} %get-tuple-element.18), channel_id=1, replica_groups=mesh['dp'=16,'tensor'=8] {'tensor'}, use_global_device_ids=true, to_apply=%add | all-reduce | flops 512 | bytes 4096 | tf_op jit(solution)/shard_map/eq | solution.py:33
  369.3 0.2 fusion.20
  369.5 1.9 fusion.8
  371.4 3.2 copy-done.1
  374.6 1.8 fusion.7
  376.4 14.8 %fusion.10 = bf16[512,1024]{1,0:T(8,128)(2,1)S(1)} fusion(bf16[1024,8192]{0,1:T(8,128)(2,1)} %bitcast.11, bf16[1,512,8192]{2,1,0:T(8,128)(2,1)} %all-gather.2.cloned.1.call-done), kind=kOutput, calls=%fused_computation.17 | convolution fusion | flops 8590458880 | bytes 26214400 | tf_op jit(solution)/shard_map/rte,he->rth/dot_general | solution.py:50
  391.3 1.3 fusion.17
  392.5 2.1 copy-done.2
  394.7 2.7 convert_bitcast_fusion
  397.4 0.5 copy-done.3
  397.9 2.0 copy-done.4
  399.8 0.8 convolution_convert_fusion.1
  400.6 15.1 %convolution_convert_fusion = bf16[1024,8192]{1,0:T(8,128)(2,1)} fusion(bf16[512,1024]{0,1:T(8,128)(2,1)S(1)} %bitcast.146, bf16[1,512,8192]{2,1,0:T(8,128)(2,1)} %all-gather.2.cloned.1.call-done), kind=kOutput, calls=%fused_computation | convolution fusion | flops 8598323200 | bytes 26214400 | tf_op jit(solution)/shard_map/rth,rte->he/dot_general | solution.py:53
  415.8 8.1 %copy.40 = bf16[8,512,512]{2,0,1:T(8,128)(2,1)} copy(bf16[8,512,512]{1,2,0:T(8,128)(2,1)} %copy-done.4) | data formatting | bytes 8388608 | tf_op jit(solution)/shard_map/reshape.42
  423.9 9.9 %fusion.9 = bf16[8,512,512]{1,2,0:T(8,128)(2,1)S(1)} fusion(f32[512,8,512]{0,2,1:T(8,128)} %copy-done.3, f32[8,512]{1,0:T(8,128)S(1)} %get-tuple-element.17, f32[8,512]{1,0:T(8,128)S(1)} %fusion.7, f32[8,512]{1,0:T(8,128)S(1)} %get-tuple-element.20, f32[512,512,8]{1,0,2:T(8,128)} %copy-done.1, pred[512,512]{0,1:T(8,128)(4,1)S(1)} %fusion.20), kind=kLoop, calls=%fused_computation.14 | loop fusion | flops 16777216 | bytes 21282816 | tf_op jit(solution)/shard_map/reshape.36
  433.8 2.2 copy-done.5
  436.0 0.8 convolution_convert_fusion.2
  436.8 1.3 copy.43
  438.1 0.3 copy.53
  438.4 3.7 fusion.15
  442.1 0.8 copy.44
  442.9 4.9 fusion.16
  447.8 115.1 %reduce-scatter.2.cloned.1.call-done = bf16[1024,512]{1,0:T(8,128)(2,1)} async-done(((bf16[1024,8192]{1,0:T(8,128)(2,1)}), bf16[1024,512]{1,0:T(8,128)(2,1)}) %reduce-scatter.2.cloned.1.call-update) | async-done | bytes 1048592 | tf_op jit(solution)/shard_map/reduce_scatter | solution.py:54
  562.9 2.8 convert_element_type.89
  (28 shorter events, 0.2 us)
Async XLA Ops:
  7.2 362.3 %copy-start = (bf16[1,512,128]{2,1,0:T(8,128)(2,1)S(1)}, bf16[1,512,128]{2,1,0:T(8,128)(2,1)}, u32[]{:S(2)}) copy-start(bf16[1,512,128]{2,1,0:T(8,128)(2,1)} %param.8) | copy-start | bytes 393220
  14.7 9.5 %copy-start.10 = (f32[1,4]{1,0:T(1,128)S(1)}, f32[1,4]{1,0:T(1,128)}, u32[]{:S(2)}) copy-start(f32[1,4]{1,0:T(1,128)} %param.11) | copy-start | bytes 52
  14.7 9.5 %copy-start.11 = (u32[128]{0:T(128)S(1)}, u32[128]{0:T(128)}, u32[]{:S(2)}) copy-start(u32[128]{0:T(128)} %constant.49) | copy-start | bytes 1540
  14.7 10.8 %copy-start.9 = (s32[1,64]{1,0:T(1,128)S(1)}, s32[1,64]{1,0:T(1,128)}, u32[]{:S(2)}) copy-start(s32[1,64]{1,0:T(1,128)} %param.10) | copy-start | bytes 772
  14.7 11.0 %copy-start.6 = (bf16[1,64,8192]{2,1,0:T(8,128)(2,1)S(1)}, bf16[1,64,8192]{2,1,0:T(8,128)(2,1)}, u32[]{:S(2)}) copy-start(bf16[1,64,8192]{2,1,0:T(8,128)(2,1)} %param.12) | copy-start | bytes 3145732
  14.7 12.3 %copy-start.7 = (bf16[1,512,1024]{2,1,0:T(8,128)(2,1)S(1)}, bf16[1,512,1024]{2,1,0:T(8,128)(2,1)}, u32[]{:S(2)}) copy-start(bf16[1,512,1024]{2,1,0:T(8,128)(2,1)} %param.7) | copy-start | bytes 3145732
  14.7 361.7 %all-to-all-start = ((bf16[16,1024,512]{1,2,0:T(8,128)(2,1)}), bf16[16,1024,512]{1,2,0:T(8,128)(2,1)}, u32[]{:S(2)}, u32[]{:S(2)}) async-start(bf16[16,1024,512]{1,2,0:T(8,128)(2,1)} %stack.2), calls=%async_computation | async-start | bytes 33554432 | tf_op jit(solution)/shard_map/all_to_all | solution.py:27
  24.1 352.3 %all-gather.2.cloned.1.call-start = ((), (), s32[]{:S(2)}) async-start(), calls=%async_computation.2 | async-start | bytes 9437184 | tf_op jit(solution)/shard_map/all_gather | solution.py:49
  26.9 536.0 %reduce-scatter.2.cloned.1.call-start = ((), (), s32[]{:S(2)}) async-start(), calls=%async_computation.3 | async-start | bytes 17825792 | tf_op jit(solution)/shard_map/reduce_scatter | solution.py:54
  371.4 3.2 copy-start.1
  376.4 14.8 %copy-start.8 = (bf16[1,512,128]{2,1,0:T(8,128)(2,1)S(1)}, bf16[1,512,128]{2,1,0:T(8,128)(2,1)}, u32[]{:S(2)}) copy-start(bf16[1,512,128]{2,1,0:T(8,128)(2,1)} %param.9) | copy-start | bytes 393220
  391.3 3.4 copy-start.2
  394.7 3.2 copy-start.3
  397.9 2.0 copy-start.4
  433.8 2.2 copy-start.5
Sparse Core Ops, SparseCore 0:
  27.2 327.0 all-gather.1
  415.9 146.9 reduce-scatter.1
